TPU v7x, 32 devices: a whole 2x2x4 slice. The times are simulated.
32 devices in a mesh: rep: 2 (over x), member: 4 (over y, core), tp: 4 (over z).
Axes of the slice: x: 2, y: 2, z: 4, core: 2. Of those that a mesh axis runs over, the one named last changes fastest.
Arguments:
- states: bfloat16 [4096, 1024], P(('rep', 'member', 'tp')), parts along dimension 0, may hold values from -6 to 6
- member_of: int32 [4096, 1], P(('rep', 'member', 'tp')), parts along dimension 0, may hold values from 0 to 1; in each aligned block of 128 rows (0 to 127, 128 to 255, ...) at most 128 rows name the same one
- place: int32 [4096], P(('rep', 'member', 'tp')), parts along dimension 0, may hold values from 0 to 2047, as said below
- norm_gain: float32 [2, 1024], replicated, may hold values from 0.5 to 2
- w_up: bfloat16 [4, 1024, 2048], P('member', None, 'tp'), may hold values from -0.1875 to 0.1875
- w_down: bfloat16 [4, 2048, 1024], P('member', 'tp'), may hold values from -0.09375 to 0.09375
- policy_gain: float32 [1024], replicated, may hold values from 0.5 to 2
- w_policy: bfloat16 [1024, 128], replicated, may hold values from -0.1875 to 0.1875
Outputs:
- imagined: bfloat16 [4096, 1024], P(('rep', 'member', 'tp')), parts along dimension 0
- action: bfloat16 [4096, 128], P(('rep', 'member', 'tp')), parts along dimension 0
There are 2 independent parts, one for each index of `rep`. A program takes and returns all parts, laid end to end along the dimension named above; an argument that names none is the same for every part. Nothing has to cross between parts.
Inputs may be any that keep to these rules, and one draw needn't show every extreme that they name: `member_of`: at most 128 of the rows of one device name any one member, and that count is reached on some device. `place`: A permutation of the 2048 learner positions; learner device k holds positions k * 128 to (k + 1) * 128 - 1, and the rows of each device go exactly 8 to every learner device.
All inputs are finite; a program needn't handle non-finite values.
Results may differ from a plain program's by a relative error of at most 0.0069.
Values may be sent and summed in bfloat16 or wider, within the bound.
A program may use at most 128 MiB of HBM per device.

v0:
```python
import jax
import jax.numpy as jnp
from jax import lax
from jax.sharding import PartitionSpec as P


def from_partner(value, axis, distance):
    return lax.ppermute(value, axis, [(i, i ^ 1 << distance) for i in range(lax.axis_size(axis))])


def rms_scale(values, gain):
    mean_square = jnp.mean(values * values, axis=-1, keepdims=True)
    return values * lax.rsqrt(mean_square + 1e-06) * gain


def running_rank(member_hits):
    return jnp.sum((jnp.cumsum(member_hits, axis=0) - member_hits) * member_hits, axis=1)


def local(states, member_of, place, norm_gain, w_up, w_down, policy_gain, w_policy):
    n_member = lax.axis_size("member")
    n_tp = lax.axis_size("tp")
    n_dev = n_member * n_tp
    group_width = 2 * n_tp
    member_total = n_member // 2
    rows_here = states.shape[0]
    feature_width = states.shape[1]
    slot_count = 2 * rows_here // n_dev
    member = member_of[:, 0]
    member_hits = (member[:, None] == jnp.arange(member_total, dtype=jnp.int32)[None, :]).astype(
        jnp.int32
    )
    earlier = running_rank(member_hits)
    target = (member * group_width + earlier % group_width) * slot_count + earlier // group_width
    picker = (jnp.arange(n_dev * slot_count, dtype=jnp.int32)[:, None] == target[None, :]).astype(
        jnp.bfloat16
    )
    outgoing = jnp.dot(picker, states, preferred_element_type=jnp.float32).astype(jnp.bfloat16)
    arrived = lax.all_to_all(
        outgoing.reshape(n_dev, slot_count, feature_width),
        ("member", "tp"),
        split_axis=0,
        concat_axis=0,
        tiled=True,
    )
    arrived = arrived.reshape(n_dev * slot_count, feature_width)
    arrived_count = arrived.shape[0]
    own_member = lax.axis_index("member") // 2
    gain_here = lax.dynamic_index_in_dim(norm_gain, own_member, 0, keepdims=False)
    normed = rms_scale(arrived.astype(jnp.float32), gain_here).astype(jnp.bfloat16)
    partner_normed = from_partner(normed, "member", 0)
    both_rows = jnp.concatenate([normed, partner_normed], axis=0)
    up_local = w_up[0]
    down_local = w_down[0]
    hidden = jax.nn.gelu(
        jnp.dot(
            lax.all_gather(both_rows, "tp", axis=0, tiled=True),
            up_local,
            preferred_element_type=jnp.float32,
        )
    ).astype(jnp.bfloat16)
    half_change = lax.psum_scatter(
        jnp.dot(hidden, down_local, preferred_element_type=jnp.float32),
        "tp",
        scatter_dimension=0,
        tiled=True,
    )
    partner_part = from_partner(half_change[arrived_count:], "member", 0)
    change = half_change[:arrived_count] + partner_part
    predicted = (arrived.astype(jnp.float32) + change).astype(jnp.bfloat16)
    returned = lax.all_to_all(
        predicted.reshape(n_dev, slot_count, feature_width),
        ("member", "tp"),
        split_axis=0,
        concat_axis=0,
        tiled=True,
    )
    returned = returned.reshape(n_dev * slot_count, feature_width)
    own_rows = jnp.einsum("sr,sd->rd", picker, returned, preferred_element_type=jnp.float32).astype(
        jnp.bfloat16
    )
    per_learner = rows_here // n_dev
    learner = place // rows_here
    spot_index = place % rows_here
    learner_hits = (learner[:, None] == jnp.arange(n_dev, dtype=jnp.int32)[None, :]).astype(
        jnp.int32
    )
    lane_index = learner * per_learner + running_rank(learner_hits)
    placer = jnp.arange(rows_here, dtype=jnp.int32)[:, None] == lane_index[None, :]
    packed = jnp.dot(
        placer.astype(jnp.bfloat16), own_rows, preferred_element_type=jnp.float32
    ).astype(jnp.bfloat16)
    packed_spot = jnp.sum(placer.astype(jnp.int32) * spot_index[None, :], axis=1)
    arrivals, arrival_spots = (
        lax.all_to_all(
            packed.reshape(n_dev, per_learner, feature_width),
            ("member", "tp"),
            split_axis=0,
            concat_axis=0,
            tiled=True,
        ),
        lax.all_to_all(
            packed_spot.reshape(n_dev, per_learner),
            ("member", "tp"),
            split_axis=0,
            concat_axis=0,
            tiled=True,
        ),
    )
    arrivals = arrivals.reshape(rows_here, feature_width)
    arrival_spots = arrival_spots.reshape(rows_here)
    settle = (jnp.arange(rows_here, dtype=jnp.int32)[:, None] == arrival_spots[None, :]).astype(
        jnp.bfloat16
    )
    imagined = jnp.dot(settle, arrivals, preferred_element_type=jnp.float32).astype(jnp.bfloat16)
    policy_normed = rms_scale(imagined.astype(jnp.float32), policy_gain).astype(jnp.bfloat16)
    action = jnp.tanh(jnp.dot(policy_normed, w_policy, preferred_element_type=jnp.float32)).astype(
        jnp.bfloat16
    )
    return (imagined, action)


def solution(mesh):
    in_specs = (
        P(("rep", "member", "tp"), None),
        P(("rep", "member", "tp"), None),
        P(("rep", "member", "tp")),
        P(),
        P("member", None, "tp"),
        P("member", "tp", None),
        P(),
        P(),
    )
    out_specs = (P(("rep", "member", "tp"), None), P(("rep", "member", "tp"), None))
    return jax.shard_map(local, mesh=mesh, in_specs=in_specs, out_specs=out_specs, check_vma=False)
```

profile of v0, /device:TPU:0, one launch (start us, length us, event | category | flops | bytes accessed | tf_op | source)
XLA Modules:
  0.0 330.6 jit_solution(9997030250772812439)
XLA Ops:
  7.2 0.0 copy-start
  7.2 0.0 copy-start.2
  7.2 0.9 fusion.38
  8.1 0.2 reduce_window_sum.23
  8.3 0.8 select_reduce_fusion
  9.1 0.7 multiply_add_fusion
  9.8 2.0 convolution_convert_fusion
  11.8 7.4 %all-to-all-start.1 = ((bf16[16,16,1024]{2,1,0:T(8,128)(2,1)}), bf16[16,16,1024]{2,1,0:T(8,128)(2,1)S(1)}, u32[]{:S(2)}, u32[]{:S(2)}) async-start(bf16[16,16,1024]{2,1,0:T(8,128)(2,1)} %bitcast.2), calls=%async_computation.1 | async-start | bytes 1048576 | tf_op jit(solution)/shard_map/all_to_all | solution.py:39
  19.2 0.0 all-gather.2.cloned.1.call-start
  19.3 0.7 constant_dynamic-slice_fusion
  20.0 14.9 %all-to-all-done.1 = bf16[16,16,1024]{2,1,0:T(8,128)(2,1)S(1)} async-done(((bf16[16,16,1024]{2,1,0:T(8,128)(2,1)}), bf16[16,16,1024]{2,1,0:T(8,128)(2,1)S(1)}, u32[]{:S(2)}, u32[]{:S(2)}) %all-to-all-start.1) | async-done | bytes 524320 | tf_op jit(solution)/shard_map/all_to_all | solution.py:39
  34.9 0.2 fusion.25
  35.1 0.1 rsqrt.20
  35.1 0.2 fusion.27
  35.3 0.1 collective-permute-start
  35.4 1.9 collective-permute-done
  37.3 1.1 pad_maximum_fusion
  38.4 0.0 all-gather.2.cloned.1.call-update
  38.4 0.0 reduce-scatter.2.cloned.1.call-start
  38.5 79.5 %all-gather.2.cloned.1.call-done = bf16[2048,1024]{1,0:T(8,128)(2,1)} async-done(((bf16[512,1024]{1,0:T(8,128)(2,1)}), bf16[2048,1024]{1,0:T(8,128)(2,1)}) %all-gather.2.cloned.1.call-update) | async-done | bytes 4194320 | tf_op jit(solution)/shard_map/all_gather | solution.py:57
  118.0 0.0 copy-done
  118.0 0.0 copy-done.2
  118.0 10.6 %fusion.8 = f32[2048,1024]{1,0:T(8,128)} fusion(bf16[1,512,1024]{2,1,0:T(8,128)(2,1)S(1)} %copy-done, bf16[2048,1024]{1,0:T(8,128)(2,1)} %all-gather.2.cloned.1.call-done, bf16[1,1024,512]{2,1,0:T(8,128)(2,1)S(1)} %copy-done.2), kind=kOutput, calls=%fused_computation.9 | convolution fusion | flops 4304404480 | bytes 14680064 | tf_op jit(solution)/shard_map/dot_general | solution.py:63
  128.6 0.0 reduce-scatter.2.cloned.1.call-update
  128.6 0.0 copy-start.5
  128.6 0.0 copy-start.3
  128.6 0.0 copy-start.4
  128.7 143.1 %reduce-scatter.2.cloned.1.call-done = f32[512,1024]{1,0:T(8,128)} async-done(((f32[2048,1024]{1,0:T(8,128)}), f32[512,1024]{1,0:T(8,128)}) %reduce-scatter.2.cloned.1.call-update) | async-done | bytes 2097168 | tf_op jit(solution)/shard_map/reduce_scatter | solution.py:62
  271.8 1.3 slice.9
  273.1 0.1 collective-permute-start.1
  273.2 2.6 collective-permute-done.1
  275.9 2.2 fusion.17
  278.1 5.4 %all-to-all-start.2 = ((bf16[16,16,1024]{2,1,0:T(8,128)(2,1)}), bf16[16,16,1024]{2,1,0:T(8,128)(2,1)S(1)}, u32[]{:S(2)}, u32[]{:S(2)}) async-start(bf16[16,16,1024]{2,1,0:T(8,128)(2,1)} %bitcast.7), calls=%async_computation.3 | async-start | bytes 1048576 | tf_op jit(solution)/shard_map/all_to_all | solution.py:71
  283.5 0.0 copy-done.5
  283.5 0.1 fusion.39
  283.6 0.2 reduce_window_sum.22
  283.8 0.2 select_reduce_fusion.2
  284.0 0.1 select_reduce_fusion.1
  284.1 0.7 all_to_all.15
  284.8 14.4 %all-to-all-done.2 = bf16[16,16,1024]{2,1,0:T(8,128)(2,1)S(1)} async-done(((bf16[16,16,1024]{2,1,0:T(8,128)(2,1)}), bf16[16,16,1024]{2,1,0:T(8,128)(2,1)S(1)}, u32[]{:S(2)}, u32[]{:S(2)}) %all-to-all-start.2) | async-done | bytes 524320 | tf_op jit(solution)/shard_map/all_to_all | solution.py:71
  299.2 3.5 %all-to-all-start = ((s32[16,1,8]{2,1,0:T(1,128)}), s32[16,1,8]{2,1,0:T(1,128)S(1)}, u32[]{:S(2)}, u32[]{:S(2)}) async-start(s32[16,1,8]{2,1,0:T(1,128)} %bitcast), calls=%async_computation | async-start | bytes 16384 | tf_op jit(solution)/shard_map/all_to_all | solution.py:102
  302.7 1.1 fusion.14
  303.8 5.1 %all-to-all-done = s32[16,1,8]{2,1,0:T(1,128)S(1)} async-done(((s32[16,1,8]{2,1,0:T(1,128)}), s32[16,1,8]{2,1,0:T(1,128)S(1)}, u32[]{:S(2)}, u32[]{:S(2)}) %all-to-all-start) | async-done | bytes 544 | tf_op jit(solution)/shard_map/all_to_all | solution.py:102
  308.9 3.5 %all-to-all-start.3 = ((bf16[16,8,1024]{2,1,0:T(8,128)(2,1)}), bf16[16,8,1024]{2,1,0:T(8,128)(2,1)S(1)}, u32[]{:S(2)}, u32[]{:S(2)}) async-start(bf16[16,8,1024]{2,1,0:T(8,128)(2,1)} %fusion.14), calls=%async_computation.4 | async-start | bytes 524288 | tf_op jit(solution)/shard_map/all_to_all | solution.py:95
  312.5 0.5 broadcast.140
  313.0 0.7 reduce.4
  313.6 0.1 eq.77
  313.7 8.7 %all-to-all-done.3 = bf16[16,8,1024]{2,1,0:T(8,128)(2,1)S(1)} async-done(((bf16[16,8,1024]{2,1,0:T(8,128)(2,1)}), bf16[16,8,1024]{2,1,0:T(8,128)(2,1)S(1)}, u32[]{:S(2)}, u32[]{:S(2)}) %all-to-all-start.3) | async-done | bytes 262176 | tf_op jit(solution)/shard_map/all_to_all | solution.py:95
  322.5 0.3 fusion.28
  322.8 0.0 copy-start.1
  322.8 0.0 copy-done.3
  322.8 0.0 copy-done.4
  322.8 0.9 fusion.15
  323.7 0.0 copy-done.1
  (4 shorter events, 0.0 us)
Async XLA Ops:
  7.2 110.8 %copy-start = (bf16[1,512,1024]{2,1,0:T(8,128)(2,1)S(1)}, bf16[1,512,1024]{2,1,0:T(8,128)(2,1)}, u32[]{:S(2)}) copy-start(bf16[1,512,1024]{2,1,0:T(8,128)(2,1)} %param.13) | copy-start | bytes 3145732
  7.2 110.8 %copy-start.2 = (bf16[1,1024,512]{2,1,0:T(8,128)(2,1)S(1)}, bf16[1,1024,512]{2,1,0:T(8,128)(2,1)}, u32[]{:S(2)}) copy-start(bf16[1,1024,512]{2,1,0:T(8,128)(2,1)} %param.12) | copy-start | bytes 3145732
  11.8 23.1 %all-to-all-start.1 = ((bf16[16,16,1024]{2,1,0:T(8,128)(2,1)}), bf16[16,16,1024]{2,1,0:T(8,128)(2,1)S(1)}, u32[]{:S(2)}, u32[]{:S(2)}) async-start(bf16[16,16,1024]{2,1,0:T(8,128)(2,1)} %bitcast.2), calls=%async_computation.1 | async-start | bytes 1048576 | tf_op jit(solution)/shard_map/all_to_all | solution.py:39
  19.2 98.8 %all-gather.2.cloned.1.call-start = ((), (), s32[]{:S(2)}) async-start(), calls=%async_computation.5 | async-start | bytes 5242880 | tf_op jit(solution)/shard_map/all_gather | solution.py:57
  35.3 2.0 collective-permute-start
  38.4 233.4 %reduce-scatter.2.cloned.1.call-start = ((), (), s32[]{:S(2)}) async-start(), calls=%async_computation.6 | async-start | bytes 10485760 | tf_op jit(solution)/shard_map/reduce_scatter | solution.py:62
  128.6 154.9 %copy-start.5 = (s32[128]{0:T(128)S(1)}, s32[128]{0:T(128)}, u32[]{:S(2)}) copy-start(s32[128]{0:T(128)} %param.10) | copy-start | bytes 1540
  128.6 194.2 %copy-start.3 = (bf16[1024,128]{1,0:T(8,128)(2,1)S(1)}, bf16[1024,128]{1,0:T(8,128)(2,1)}, u32[]{:S(2)}) copy-start(bf16[1024,128]{1,0:T(8,128)(2,1)} %param.15) | copy-start | bytes 786436
  128.6 194.2 %copy-start.4 = (f32[1024]{0:T(1024)S(1)}, f32[1024]{0:T(1024)}, u32[]{:S(2)}) copy-start(f32[1024]{0:T(1024)} %param.14) | copy-start | bytes 12292
  273.1 2.7 collective-permute-start.1
  278.1 21.1 %all-to-all-start.2 = ((bf16[16,16,1024]{2,1,0:T(8,128)(2,1)}), bf16[16,16,1024]{2,1,0:T(8,128)(2,1)S(1)}, u32[]{:S(2)}, u32[]{:S(2)}) async-start(bf16[16,16,1024]{2,1,0:T(8,128)(2,1)} %bitcast.7), calls=%async_computation.3 | async-start | bytes 1048576 | tf_op jit(solution)/shard_map/all_to_all | solution.py:71
  299.2 9.7 %all-to-all-start = ((s32[16,1,8]{2,1,0:T(1,128)}), s32[16,1,8]{2,1,0:T(1,128)S(1)}, u32[]{:S(2)}, u32[]{:S(2)}) async-start(s32[16,1,8]{2,1,0:T(1,128)} %bitcast), calls=%async_computation | async-start | bytes 16384 | tf_op jit(solution)/shard_map/all_to_all | solution.py:102
  308.9 13.6 %all-to-all-start.3 = ((bf16[16,8,1024]{2,1,0:T(8,128)(2,1)}), bf16[16,8,1024]{2,1,0:T(8,128)(2,1)S(1)}, u32[]{:S(2)}, u32[]{:S(2)}) async-start(bf16[16,8,1024]{2,1,0:T(8,128)(2,1)} %fusion.14), calls=%async_computation.4 | async-start | bytes 524288 | tf_op jit(solution)/shard_map/all_to_all | solution.py:95
  322.8 1.0 copy-start.1
Sparse Core Ops, SparseCore 0:
  38.5 79.4 all-gather.1
  128.7 143.0 reduce-scatter.1
where the time goes:
time: 331 us
  waiting for transfers between devices  270 us (82%)
  starting transfers between devices  20 us (6%)
  matrix products  15 us (5%)
  between operations  14.3 us (4%)
  other arithmetic  7.45 us (2%)
  local copies, waits for them, and re-layouts  3.45 us (1%)
    reduce_scatter x1, waiting for transfers between devices, local(): lax.psum_scatter(jnp.dot(hidden, down_local, preferred_element_type=jnp.f...  143 us
    all_gather x1, waiting for transfers between devices, local(): lax.all_gather(both_rows, 'tp', axis=0, tiled=True)  79.5 us
    all_to_all x1, waiting for transfers between devices, local(): lax.all_to_all(outgoing.reshape(n_dev, slot_count, feature_width), ('memb...  14.9 us
    all_to_all x1, waiting for transfers between devices, local(): lax.all_to_all(predicted.reshape(n_dev, slot_count, feature_width), ('mem...  14.4 us
    dot_general x1, matrix products, local(): jnp.dot(hidden, down_local, preferred_element_type=jnp.float32)  10.6 us
    all_to_all x1, waiting for transfers between devices, local(): lax.all_to_all(packed.reshape(n_dev, per_learner, feature_width), ('membe...  8.74 us
    all_to_all x1, starting transfers between devices, local(): lax.all_to_all(outgoing.reshape(n_dev, slot_count, feature_width), ('memb...  7.39 us
  transfers between devices with their start and end apart: 8, of which 8 were waited for; matrix products, arithmetic and copies ran while one was open for 1% of the time, Pallas kernels for 0%

commit v1 on v0

--- a/solution.py
+++ b/solution.py
@@ -1,6 +1,8 @@
 import jax
 import jax.numpy as jnp
 from jax import lax
+from jax.experimental import pallas as pl
+from jax.experimental.pallas import tpu as pltpu
 from jax.sharding import PartitionSpec as P
 
 
@@ -17,7 +19,7 @@
     return jnp.sum((jnp.cumsum(member_hits, axis=0) - member_hits) * member_hits, axis=1)
 
 
-def local(states, member_of, place, norm_gain, w_up, w_down, policy_gain, w_policy):
+def dispatched(states, member_of, place, norm_gain, w_up, w_down, policy_gain, w_policy):
     n_member = lax.axis_size("member")
     n_tp = lax.axis_size("tp")
     n_dev = n_member * n_tp
@@ -120,6 +122,359 @@
     return (imagined, action)
 
 
+RIGHT, LEFT, ACROSS, SIBLING = range(4)
+
+
+def near_order(z):
+    return (
+        z,
+        z - 1 + 2 * ((3 - z) // 3),
+        2 + z // 2 - 2 * (z // 3),
+        3 - 3 * (z // 2),
+    )
+
+
+def rollout_kernel(
+    states_ref,
+    member_ref,
+    place_ref,
+    gain_ref,
+    up_ref,
+    down_ref,
+    policy_gain_ref,
+    policy_ref,
+    imagined_ref,
+    action_ref,
+    rows,
+    notes,
+    parts,
+    sibling_parts,
+    sums,
+    across_parts,
+    from_left,
+    from_right,
+    outgoing,
+    total,
+    gather_send,
+    gather_recv,
+    part_send,
+    part_recv,
+    across_send,
+    across_recv,
+    line_send,
+    left_recv,
+    right_recv,
+):
+    width = states_ref.shape[1]
+    z = lax.axis_index("tp")
+    m = lax.axis_index("member")
+    y = m // 2
+    h = m % 2
+    chip = y * 4 + z
+    targets = {
+        RIGHT: {"tp": z + 1},
+        LEFT: {"tp": z - 1},
+        ACROSS: {"member": m + 2 - 4 * y},
+        SIBLING: {"member": m + 1 - 2 * h},
+    }
+    has_right = z < 3
+    has_left = z > 0
+    order = near_order(z)
+
+    def greet(way):
+        pl.semaphore_signal(
+            barrier, inc=1, device_id=targets[way], device_id_type=pl.DeviceIdType.MESH
+        )
+
+    def remote(source, target, send_sem, recv_sem, way):
+        return pltpu.make_async_remote_copy(
+            src_ref=source,
+            dst_ref=target,
+            send_sem=send_sem,
+            recv_sem=recv_sem,
+            device_id=targets[way],
+            device_id_type=pl.DeviceIdType.MESH,
+        )
+
+    barrier = pltpu.get_barrier_semaphore()
+    greet(ACROSS)
+    greet(SIBLING)
+    pl.when(has_right)(lambda: greet(RIGHT))
+    pl.when(has_left)(lambda: greet(LEFT))
+
+    lane = lax.broadcasted_iota(jnp.int32, (128, 128), 1)
+    sub = lax.broadcasted_iota(jnp.int32, (128, 128), 0)
+    place_row = place_ref[...]
+    learner = place_row >> 7
+    spot = place_row & 127
+    key_row = ((((learner >> 3) << 2) + (learner & 3)) << 1) + ((learner >> 2) & 1)
+    rank_row = key_row * 128 + lax.broadcasted_iota(jnp.int32, (1, 128), 1)
+    rank_col = jnp.sum(jnp.where(lane == sub, rank_row, 0), axis=1, keepdims=True)
+    sorted_row = jnp.sum((rank_col < rank_row).astype(jnp.int32), axis=0, keepdims=True)
+    picker = (sub == sorted_row).astype(jnp.bfloat16)
+    member_row = jnp.sum(jnp.where(lane == sub, member_ref[...], 0), axis=0, keepdims=True)
+    line = lax.broadcasted_iota(jnp.int32, (16, 128), 0)
+    facts = jnp.where(line == 0, member_row, jnp.where(line == 1, spot, 0))
+    own_notes = lax.dot_general(
+        facts.astype(jnp.bfloat16),
+        picker,
+        (((1,), (1,)), ((), ())),
+        preferred_element_type=jnp.float32,
+    )
+    notes[chip, h] = own_notes[:8]
+    rows[chip, h] = jnp.dot(
+        picker, states_ref[...], preferred_element_type=jnp.float32
+    ).astype(jnp.bfloat16)
+
+    pl.semaphore_wait(barrier, 2 + (z + 2) // 3 + (5 - z) // 3)
+
+    def block(way, at):
+        return [
+            remote(
+                buffer.at[at, h],
+                buffer.at[at, h],
+                gather_send.at[kind, way, at],
+                gather_recv.at[kind, at, h],
+                way,
+            )
+            for kind, buffer in enumerate((notes, rows))
+        ]
+
+    def send_block(way, at):
+        for copy in block(way, at):
+            copy.start()
+
+    def await_block(at, core):
+        for kind, buffer in enumerate((notes, rows)):
+            remote(
+                buffer.at[at, core],
+                buffer.at[at, core],
+                gather_send.at[kind, SIBLING, at],
+                gather_recv.at[kind, at, core],
+                SIBLING,
+            ).wait_recv()
+
+    gain = gain_ref[pl.ds(y, 1), :]
+
+    def part(at):
+        return remote(
+            parts.at[at, 1 - h],
+            sibling_parts.at[at],
+            part_send.at[at],
+            part_recv.at[at],
+            SIBLING,
+        )
+
+    def predict(at):
+        base = jnp.concatenate([rows[at, 0], rows[at, 1]], axis=0).astype(jnp.float32)
+        kept = jnp.concatenate(
+            [
+                jnp.sum(
+                    jnp.where((lane == sub) & (notes[at, core][0:1] == y.astype(jnp.float32)), 1.0, 0.0),
+                    axis=1,
+                    keepdims=True,
+                )
+                for core in range(2)
+            ],
+            axis=0,
+        )
+        mean_square = jnp.mean(base * base, axis=-1, keepdims=True)
+        normed = (base * (lax.rsqrt(mean_square + 1e-06) * kept) * gain).astype(jnp.bfloat16)
+        wide = jnp.dot(normed, up_ref[0], preferred_element_type=jnp.float32)
+        wide = 0.5 * wide * (1.0 + jnp.tanh(0.7978845608028654 * (wide + 0.044715 * (wide * wide * wide))))
+        hidden = jnp.concatenate(
+            [
+                wide[source * 128 + target * 16 + core * 8 :][:8]
+                for core in range(2)
+                for target in range(8)
+                for source in range(2)
+            ],
+            axis=0,
+        ).astype(jnp.bfloat16)
+        change = jnp.dot(hidden, down_ref[0], preferred_element_type=jnp.float32)
+        change = change.astype(jnp.bfloat16)
+        parts[at, 0] = change[:128]
+        parts[at, 1] = change[128:]
+        part(at).start()
+
+    def combine(at):
+        part(at).wait_recv()
+        both = parts[at, h].astype(jnp.float32) + sibling_parts[at].astype(jnp.float32)
+        sums[:, pl.ds(pl.multiple_of(at * 16, 16), 16), :] = both.astype(jnp.bfloat16).reshape(
+            8, 16, width
+        )
+
+    waiting = []
+    for step in range(5):
+        ready = []
+        if step < 4:
+            at = y * 4 + order[step]
+            if step > 0:
+                await_block(at, h)
+            pl.when(has_right & (order[step] <= z))(lambda: send_block(RIGHT, at))
+            pl.when(has_left & (order[step] >= z))(lambda: send_block(LEFT, at))
+            send_block(ACROSS, at)
+            send_block(SIBLING, at)
+            ready.append((at, False))
+        if step > 0:
+            ready.append(((1 - y) * 4 + order[step - 1], True))
+        for unit, crossed in ready:
+            if crossed:
+                await_block(unit, h)
+                send_block(SIBLING, unit)
+            await_block(unit, 1 - h)
+            predict(unit)
+            if waiting:
+                combine(waiting.pop())
+            waiting.append(unit)
+    combine(waiting.pop())
+
+    def across(to):
+        return remote(
+            sums.at[(1 - y) * 4 + to],
+            across_parts.at[to],
+            across_send.at[to],
+            across_recv.at[to],
+            ACROSS,
+        )
+
+    def along(to, way):
+        arrivals, recv = (from_left, left_recv) if way == RIGHT else (from_right, right_recv)
+        return remote(
+            outgoing.at[to], arrivals.at[to], line_send.at[to], recv.at[to], way
+        )
+
+    for step in range(4):
+        across(order[3 - step]).start()
+    for step in range(3):
+        to = order[3 - step]
+        across(to).wait_recv()
+
+        def pass_on(way, arrivals, chained):
+            def start():
+                own = sums[y * 4 + to].astype(jnp.float32) + across_parts[to].astype(jnp.float32)
+                outgoing[to] = own.astype(jnp.bfloat16)
+                along(to, way).start()
+
+            def go_on():
+                along(to, way).wait_recv()
+                own = sums[y * 4 + to].astype(jnp.float32) + across_parts[to].astype(jnp.float32)
+                outgoing[to] = (own + arrivals[to].astype(jnp.float32)).astype(jnp.bfloat16)
+                along(to, way).start()
+
+            pl.when(chained)(go_on)
+            pl.when(jnp.logical_not(chained))(start)
+
+        pl.when(to > z)(lambda: pass_on(RIGHT, from_left, has_left))
+        pl.when(to < z)(lambda: pass_on(LEFT, from_right, has_right))
+    across(z).wait_recv()
+    total[...] = sums[chip].astype(jnp.float32) + across_parts[z].astype(jnp.float32)
+
+    @pl.when(has_left)
+    def _():
+        along(z, RIGHT).wait_recv()
+        total[...] += from_left[z].astype(jnp.float32)
+
+    @pl.when(has_right)
+    def _():
+        along(z, LEFT).wait_recv()
+        total[...] += from_right[z].astype(jnp.float32)
+
+    base = rows[:, :, pl.ds(pl.multiple_of(chip * 16, 16), 16), :].astype(jnp.float32)
+    base = jnp.where(h == 0, base[:, :, :8], base[:, :, 8:]).reshape(128, width)
+    predicted = (base + total[...]).astype(jnp.bfloat16)
+    spots = jnp.concatenate(
+        [notes[at, core][1:2] for at in range(8) for core in range(2)], axis=0
+    ).astype(jnp.bfloat16)
+    own_spots = (sub == chip * 16 + h * 8 + (lane & 7)).astype(jnp.bfloat16)
+    spread = jnp.dot(spots, own_spots, preferred_element_type=jnp.float32)
+    line = lax.broadcasted_iota(jnp.int32, (16, 128), 0)
+    across_lanes = lax.broadcasted_iota(jnp.int32, (16, 128), 1)
+    spot_row = jnp.sum(
+        jnp.where(line == across_lanes >> 3, spread, 0.0), axis=0, keepdims=True
+    ).astype(jnp.int32)
+    settle = (sub == spot_row).astype(jnp.bfloat16)
+    imagined = jnp.dot(settle, predicted, preferred_element_type=jnp.float32)
+    imagined_ref[...] = imagined.astype(jnp.bfloat16)
+    policy_normed = rms_scale(imagined, policy_gain_ref[...]).astype(jnp.bfloat16)
+    action_ref[...] = jnp.tanh(
+        jnp.dot(policy_normed, policy_ref[...], preferred_element_type=jnp.float32)
+    ).astype(jnp.bfloat16)
+
+    for step in range(4):
+        at = y * 4 + order[step]
+        other = (1 - y) * 4 + order[step]
+
+        def sent(way, where):
+            for copy in block(way, where):
+                copy.wait_send()
+
+        pl.when(has_right & (order[step] <= z))(lambda: sent(RIGHT, at))
+        pl.when(has_left & (order[step] >= z))(lambda: sent(LEFT, at))
+        sent(ACROSS, at)
+        sent(SIBLING, at)
+        sent(SIBLING, other)
+        part(at).wait_send()
+        part(other).wait_send()
+        across(order[step]).wait_send()
+        if step > 0:
+            along(order[step], RIGHT).wait_send()
+
+
+def gathered(states, member_of, place, norm_gain, w_up, w_down, policy_gain, w_policy):
+    count, width = states.shape
+    vmem = pl.BlockSpec(memory_space=pltpu.VMEM)
+    dma = pltpu.SemaphoreType.DMA
+    half = jnp.bfloat16
+    return pl.pallas_call(
+        rollout_kernel,
+        out_shape=(
+            jax.ShapeDtypeStruct((count, width), half),
+            jax.ShapeDtypeStruct((count, w_policy.shape[1]), half),
+        ),
+        in_specs=[vmem] * 8,
+        out_specs=(vmem, vmem),
+        scratch_shapes=[
+            pltpu.VMEM((8, 2, count, width), half),
+            pltpu.VMEM((8, 2, 8, 128), jnp.float32),
+            pltpu.VMEM((8, 2, count, width), half),
+            pltpu.VMEM((8, count, width), half),
+            pltpu.VMEM((8, count, width), half),
+            pltpu.VMEM((4, count, width), half),
+            pltpu.VMEM((4, count, width), half),
+            pltpu.VMEM((4, count, width), half),
+            pltpu.VMEM((4, count, width), half),
+            pltpu.VMEM((count, width), jnp.float32),
+            dma((2, 4, 8)),
+            dma((2, 8, 2)),
+            dma((8,)),
+            dma((8,)),
+            dma((4,)),
+            dma((4,)),
+            dma((4,)),
+            dma((4,)),
+            dma((4,)),
+        ],
+        compiler_params=pltpu.CompilerParams(
+            collective_id=0, has_side_effects=True, vmem_limit_bytes=48 * 1024 * 1024
+        ),
+        cost_estimate=pl.CostEstimate(
+            flops=2 * 2 * 16 * count * width * w_up.shape[2],
+            bytes_accessed=8 * 1024 * 1024,
+            transcendentals=16 * count * w_up.shape[2],
+        ),
+    )(
+        states,
+        member_of,
+        place.reshape(1, count),
+        norm_gain,
+        w_up,
+        w_down,
+        policy_gain.reshape(1, width),
+        w_policy,
+    )
+
+
 def solution(mesh):
     in_specs = (
         P(("rep", "member", "tp"), None),
@@ -132,4 +487,5 @@
         P(),
     )
     out_specs = (P(("rep", "member", "tp"), None), P(("rep", "member", "tp"), None))
+    local = gathered if mesh.shape["member"] == 4 and mesh.shape["tp"] == 4 else dispatched
     return jax.shard_map(local, mesh=mesh, in_specs=in_specs, out_specs=out_specs, check_vma=False)

time: 331 us -> 75.5 us (0.23)
  waiting for transfers between devices: 270 us -> 0 us
  Pallas kernels: 0 us -> 67.5 us
  starting transfers between devices: 20 us -> 0 us
  matrix products: 15 us -> 0 us
  between operations: 14.3 us -> 0.66 us
  other arithmetic: 7.45 us -> 0 us
  local copies, waits for them, and re-layouts: 3.45 us -> 7.02 us
    reduce_scatter x1 -> x0, waiting for transfers between devices: 143 us -> none  [local(): lax.psum_scatter(jnp.dot(hidden, down_local, preferred_element_type=jnp.f...]
    all_gather x1 -> x0, waiting for transfers between devices: 79.5 us -> none  [local(): lax.all_gather(both_rows, 'tp', axis=0, tiled=True)]
    pallas_call x0 -> x1, Pallas kernels: none -> 67.5 us  [gathered(): pl.pallas_call(rollout_kernel, out_shape=(jax.ShapeDtypeStruct((count, wi...]
    all_to_all x4 -> x0, waiting for transfers between devices: 43.1 us -> none  [the longest x1 14.9 us: local(): lax.all_to_all(outgoing.reshape(n_dev, slot_count, feature_width), ('memb...]
    all_to_all x4 -> x0, starting transfers between devices: 19.8 us -> none  [the longest x1 7.39 us: local(): lax.all_to_all(outgoing.reshape(n_dev, slot_count, feature_width), ('memb...]
    dot_general x5 -> x0, matrix products: 15 us -> none  [the longest x1 10.6 us: local(): jnp.dot(hidden, down_local, preferred_element_type=jnp.float32)]
    unnamed x12 -> x19, local copies, waits for them, and re-layouts: 0.04 us -> 7.02 us
    ppermute x2 -> x0, waiting for transfers between devices: 4.54 us -> none  [from_partner(): lax.ppermute(value, axis, [(i, i ^ 1 << distance) for i in range(lax.axis...]
  transfers between devices with their start and end apart: 8 -> 0, of which waited for: 8 -> 0; matrix products, arithmetic and copies ran while one was open for 1% -> 0% of each run, Pallas kernels for 0% -> 0%
where the time goes in v1:
time: 75.5 us; the launch traced here: 75.2 us
  Pallas kernels  67.5 us (89%)
  local copies, waits for them, and re-layouts  7.02 us (9%)
    pallas_call x1, Pallas kernels, gathered(): pl.pallas_call(rollout_kernel, out_shape=(jax.ShapeDtypeStruct((count, wi...  67.5 us
    unnamed x19, local copies, waits for them, and re-layouts  7.02 us

profile of v1, /device:TPU:0, one launch (start us, length us, event | category | flops | bytes accessed | tf_op | source)
XLA Modules:
  0.0 75.2 jit_solution(2985195749510682272)
XLA Ops:
  0.6 0.0 copy-start.7
  0.6 0.6 copy-done.7
  1.3 0.0 copy-start.4
  1.3 0.0 copy-start.5
  1.3 0.0 copy-start.6
  1.3 0.1 copy.10.member_ref
  1.4 0.6 copy-done.4
  2.0 0.0 copy-done.5
  2.0 0.0 copy-done.6
  2.0 0.0 copy-start
  2.0 1.2 %copy-done = bf16[1,1024,512]{2,1,0:T(8,128)(2,1)S(1)} copy-done((bf16[1,1024,512]{2,1,0:T(8,128)(2,1)S(1)}, bf16[1,1024,512]{2,1,0:T(8,128)(2,1)}, u32[]{:S(2)}) %copy-start) | copy-done | bytes 1048600
  3.2 0.0 copy-start.1
  3.2 1.2 %copy-done.1 = bf16[1,512,1024]{2,1,0:T(8,128)(2,1)S(1)} copy-done((bf16[1,512,1024]{2,1,0:T(8,128)(2,1)S(1)}, bf16[1,512,1024]{2,1,0:T(8,128)(2,1)}, u32[]{:S(2)}) %copy-start.1) | copy-done | bytes 1048600
  4.4 0.0 copy-start.2
  4.4 0.9 %copy-done.2 = bf16[128,1024]{1,0:T(8,128)(2,1)S(1)} copy-done((bf16[128,1024]{1,0:T(8,128)(2,1)S(1)}, bf16[128,1024]{1,0:T(8,128)(2,1)}, u32[]{:S(2)}) %copy-start.2) | copy-done | bytes 262168
  5.4 0.0 copy-start.3
  5.4 0.9 %copy-done.3 = bf16[1024,128]{1,0:T(8,128)(2,1)S(1)} copy-done((bf16[1024,128]{1,0:T(8,128)(2,1)S(1)}, bf16[1024,128]{1,0:T(8,128)(2,1)}, u32[]{:S(2)}) %copy-start.3) | copy-done | bytes 262168
  6.3 67.5 %shard_map.95 = (bf16[128,1024]{1,0:T(8,128)(2,1)S(1)}, bf16[128,128]{1,0:T(8,128)(2,1)S(1)}) custom-call(bf16[128,1024]{1,0:T(8,128)(2,1)S(1)} %copy-done.2, s32[128,1]{1,0:T(8,128)S(1)} %copy.10.member_ref, s32[1,128]{1,0:T(1,128)S(1)} %bitcast.3, f32[2,1024]{1,0:T(2,128)S(1)} %copy-done.4, bf16[1,1024,512]{2,1,0:T(8,128)(2,1)S(1)} %copy-done, ...), custom_call_target="tpu_custom_call" | custom-call | flops 4294967296 | bytes 8388608 | tf_op jit(solution)/shard_map/pallas_call | solution.py:429
  73.9 0.7 copy.13
  74.6 0.6 copy.14
Async XLA Ops:
  0.6 0.7 copy-start.7
  1.3 0.7 copy-start.4
  1.3 0.7 copy-start.5
  1.3 0.7 copy-start.6
  2.0 1.2 %copy-start = (bf16[1,1024,512]{2,1,0:T(8,128)(2,1)S(1)}, bf16[1,1024,512]{2,1,0:T(8,128)(2,1)}, u32[]{:S(2)}) copy-start(bf16[1,1024,512]{2,1,0:T(8,128)(2,1)} %up_ref.1) | copy-start | bytes 3145732
  3.2 1.2 %copy-start.1 = (bf16[1,512,1024]{2,1,0:T(8,128)(2,1)S(1)}, bf16[1,512,1024]{2,1,0:T(8,128)(2,1)}, u32[]{:S(2)}) copy-start(bf16[1,512,1024]{2,1,0:T(8,128)(2,1)} %down_ref.1) | copy-start | bytes 3145732
  4.4 0.9 %copy-start.2 = (bf16[128,1024]{1,0:T(8,128)(2,1)S(1)}, bf16[128,1024]{1,0:T(8,128)(2,1)}, u32[]{:S(2)}) copy-start(bf16[128,1024]{1,0:T(8,128)(2,1)} %states_ref.1) | copy-start | bytes 786436
  5.4 0.9 %copy-start.3 = (bf16[1024,128]{1,0:T(8,128)(2,1)S(1)}, bf16[1024,128]{1,0:T(8,128)(2,1)}, u32[]{:S(2)}) copy-start(bf16[1024,128]{1,0:T(8,128)(2,1)} %policy_ref.1) | copy-start | bytes 786436

commit v2 on v1

--- a/solution.py
+++ b/solution.py
@@ -135,6 +135,16 @@
 
 
 def rollout_kernel(
+    states_in,
+    member_in,
+    place_in,
+    gain_in,
+    up_in,
+    down_in,
+    policy_gain_in,
+    policy_in,
+    imagined_ref,
+    action_ref,
     states_ref,
     member_ref,
     place_ref,
@@ -143,8 +153,7 @@
     down_ref,
     policy_gain_ref,
     policy_ref,
-    imagined_ref,
-    action_ref,
+    fetch_sem,
     rows,
     notes,
     parts,
@@ -166,6 +175,23 @@
     right_recv,
 ):
     width = states_ref.shape[1]
+    fetches = [
+        pltpu.make_async_copy(source, target, fetch_sem.at[i])
+        for i, (source, target) in enumerate(
+            (
+                (place_in, place_ref),
+                (member_in, member_ref),
+                (states_in, states_ref),
+                (gain_in, gain_ref),
+                (up_in, up_ref),
+                (down_in, down_ref),
+                (policy_gain_in, policy_gain_ref),
+                (policy_in, policy_ref),
+            )
+        )
+    ]
+    for fetch in fetches:
+        fetch.start()
     z = lax.axis_index("tp")
     m = lax.axis_index("member")
     y = m // 2
@@ -202,6 +228,8 @@
     pl.when(has_right)(lambda: greet(RIGHT))
     pl.when(has_left)(lambda: greet(LEFT))
 
+    for fetch in fetches[:3]:
+        fetch.wait()
     lane = lax.broadcasted_iota(jnp.int32, (128, 128), 1)
     sub = lax.broadcasted_iota(jnp.int32, (128, 128), 0)
     place_row = place_ref[...]
@@ -228,33 +256,28 @@
 
     pl.semaphore_wait(barrier, 2 + (z + 2) // 3 + (5 - z) // 3)
 
-    def block(way, at):
-        return [
-            remote(
-                buffer.at[at, h],
-                buffer.at[at, h],
-                gather_send.at[kind, way, at],
-                gather_recv.at[kind, at, h],
-                way,
-            )
-            for kind, buffer in enumerate((notes, rows))
-        ]
-
-    def send_block(way, at):
-        for copy in block(way, at):
-            copy.start()
-
-    def await_block(at, core):
-        for kind, buffer in enumerate((notes, rows)):
-            remote(
-                buffer.at[at, core],
-                buffer.at[at, core],
-                gather_send.at[kind, SIBLING, at],
-                gather_recv.at[kind, at, core],
-                SIBLING,
-            ).wait_recv()
-
-    gain = gain_ref[pl.ds(y, 1), :]
+    def pieces(at, core):
+        return (
+            notes.at[at, core],
+            rows.at[at, core, pl.ds(0, 64)],
+            rows.at[at, core, pl.ds(64, 64)],
+        )
+
+    def piece(way, at, kind):
+        where = pieces(at, h)[kind]
+        return remote(
+            where, where, gather_send.at[kind, way, at], gather_recv.at[kind, at, h], way
+        )
+
+    def await_piece(at, core, kind):
+        where = pieces(at, core)[kind]
+        remote(
+            where,
+            where,
+            gather_send.at[kind, SIBLING, at],
+            gather_recv.at[kind, at, core],
+            SIBLING,
+        ).wait_recv()
 
     def part(at):
         return remote(
@@ -304,82 +327,109 @@
             8, 16, width
         )
 
+    def across(to, line):
+        span = pl.ds(pl.multiple_of(line * 64, 64), 64)
+        return remote(
+            sums.at[(1 - y) * 4 + to, span],
+            across_parts.at[to, span],
+            across_send.at[to, line],
+            across_recv.at[to, line],
+            ACROSS,
+        )
+
+    for fetch in fetches[3:6]:
+        fetch.wait()
+    gain = gain_ref[pl.ds(y, 1), :]
     waiting = []
     for step in range(5):
-        ready = []
         if step < 4:
             at = y * 4 + order[step]
-            if step > 0:
-                await_block(at, h)
-            pl.when(has_right & (order[step] <= z))(lambda: send_block(RIGHT, at))
-            pl.when(has_left & (order[step] >= z))(lambda: send_block(LEFT, at))
-            send_block(ACROSS, at)
-            send_block(SIBLING, at)
-            ready.append((at, False))
+            for kind in range(3):
+                if step > 0:
+                    await_piece(at, h, kind)
+                pl.when(has_right & (order[step] <= z))(lambda: piece(RIGHT, at, kind).start())
+                pl.when(has_left & (order[step] >= z))(lambda: piece(LEFT, at, kind).start())
+                piece(ACROSS, at, kind).start()
+                piece(SIBLING, at, kind).start()
+            for kind in range(3):
+                await_piece(at, 1 - h, kind)
+            predict(at)
+            waiting.append(at)
         if step > 0:
-            ready.append(((1 - y) * 4 + order[step - 1], True))
-        for unit, crossed in ready:
-            if crossed:
-                await_block(unit, h)
-                send_block(SIBLING, unit)
-            await_block(unit, 1 - h)
-            predict(unit)
-            if waiting:
-                combine(waiting.pop())
-            waiting.append(unit)
+            crossed = (1 - y) * 4 + order[step - 1]
+            for kind in range(3):
+                await_piece(crossed, h, kind)
+                piece(SIBLING, crossed, kind).start()
+            while waiting:
+                combine(waiting.pop(0))
+            if step == 3:
+                for k in range(4):
+                    across(order[3 - k], y).start()
+            for kind in range(3):
+                await_piece(crossed, 1 - h, kind)
+            predict(crossed)
+            waiting.append(crossed)
     combine(waiting.pop())
 
-    def across(to):
-        return remote(
-            sums.at[(1 - y) * 4 + to],
-            across_parts.at[to],
-            across_send.at[to],
-            across_recv.at[to],
-            ACROSS,
-        )
-
-    def along(to, way):
+    def along(to, line, way):
+        span = pl.ds(pl.multiple_of(line * 64, 64), 64)
         arrivals, recv = (from_left, left_recv) if way == RIGHT else (from_right, right_recv)
         return remote(
-            outgoing.at[to], arrivals.at[to], line_send.at[to], recv.at[to], way
-        )
-
-    for step in range(4):
-        across(order[3 - step]).start()
-    for step in range(3):
-        to = order[3 - step]
-        across(to).wait_recv()
-
-        def pass_on(way, arrivals, chained):
-            def start():
-                own = sums[y * 4 + to].astype(jnp.float32) + across_parts[to].astype(jnp.float32)
-                outgoing[to] = own.astype(jnp.bfloat16)
-                along(to, way).start()
-
-            def go_on():
-                along(to, way).wait_recv()
-                own = sums[y * 4 + to].astype(jnp.float32) + across_parts[to].astype(jnp.float32)
-                outgoing[to] = (own + arrivals[to].astype(jnp.float32)).astype(jnp.bfloat16)
-                along(to, way).start()
-
-            pl.when(chained)(go_on)
-            pl.when(jnp.logical_not(chained))(start)
-
-        pl.when(to > z)(lambda: pass_on(RIGHT, from_left, has_left))
-        pl.when(to < z)(lambda: pass_on(LEFT, from_right, has_right))
-    across(z).wait_recv()
-    total[...] = sums[chip].astype(jnp.float32) + across_parts[z].astype(jnp.float32)
-
-    @pl.when(has_left)
-    def _():
-        along(z, RIGHT).wait_recv()
-        total[...] += from_left[z].astype(jnp.float32)
-
-    @pl.when(has_right)
-    def _():
-        along(z, LEFT).wait_recv()
-        total[...] += from_right[z].astype(jnp.float32)
-
+            outgoing.at[to, span],
+            arrivals.at[to, span],
+            line_send.at[to, line],
+            recv.at[to, line],
+            way,
+        )
+
+    for k in range(2):
+        across(order[3 - k], 1 - y).start()
+    for turn, line in enumerate((1 - y, y)):
+        span = pl.ds(pl.multiple_of(line * 64, 64), 64)
+        for k in range(3):
+            to = order[3 - k]
+            across(to, line).wait_recv()
+
+            def pass_on(way, arrivals, chained):
+                def summed():
+                    own = sums[y * 4 + to, span].astype(jnp.float32)
+                    return own + across_parts[to, span].astype(jnp.float32)
+
+                def start():
+                    outgoing[to, span] = summed().astype(jnp.bfloat16)
+                    along(to, line, way).start()
+
+                def go_on():
+                    along(to, line, way).wait_recv()
+                    both = summed() + arrivals[to, span].astype(jnp.float32)
+                    outgoing[to, span] = both.astype(jnp.bfloat16)
+                    along(to, line, way).start()
+
+                pl.when(chained)(go_on)
+                pl.when(jnp.logical_not(chained))(start)
+
+            pl.when(to > z)(lambda: pass_on(RIGHT, from_left, has_left))
+            pl.when(to < z)(lambda: pass_on(LEFT, from_right, has_right))
+            if turn == 0 and k < 2:
+                across(order[3 - k], 1 - y).wait_send()
+                across(order[1 - k], 1 - y).start()
+        across(z, line).wait_recv()
+        total[span] = sums[chip, span].astype(jnp.float32) + across_parts[z, span].astype(
+            jnp.float32
+        )
+
+        @pl.when(has_left)
+        def _():
+            along(z, line, RIGHT).wait_recv()
+            total[span] += from_left[z, span].astype(jnp.float32)
+
+        @pl.when(has_right)
+        def _():
+            along(z, line, LEFT).wait_recv()
+            total[span] += from_right[z, span].astype(jnp.float32)
+
+    for fetch in fetches[6:]:
+        fetch.wait()
     base = rows[:, :, pl.ds(pl.multiple_of(chip * 16, 16), 16), :].astype(jnp.float32)
     base = jnp.where(h == 0, base[:, :, :8], base[:, :, 8:]).reshape(128, width)
     predicted = (base + total[...]).astype(jnp.bfloat16)
@@ -405,20 +455,20 @@
         at = y * 4 + order[step]
         other = (1 - y) * 4 + order[step]
 
-        def sent(way, where):
-            for copy in block(way, where):
-                copy.wait_send()
-
-        pl.when(has_right & (order[step] <= z))(lambda: sent(RIGHT, at))
-        pl.when(has_left & (order[step] >= z))(lambda: sent(LEFT, at))
-        sent(ACROSS, at)
-        sent(SIBLING, at)
-        sent(SIBLING, other)
+        for kind in range(3):
+            pl.when(has_right & (order[step] <= z))(lambda: piece(RIGHT, at, kind).wait_send())
+            pl.when(has_left & (order[step] >= z))(lambda: piece(LEFT, at, kind).wait_send())
+            piece(ACROSS, at, kind).wait_send()
+            piece(SIBLING, at, kind).wait_send()
+            piece(SIBLING, other, kind).wait_send()
         part(at).wait_send()
         part(other).wait_send()
-        across(order[step]).wait_send()
+        across(order[step], y).wait_send()
+        if step < 2:
+            across(order[step], 1 - y).wait_send()
         if step > 0:
-            along(order[step], RIGHT).wait_send()
+            for line in range(2):
+                along(order[step], line, RIGHT).wait_send()
 
 
 def gathered(states, member_of, place, norm_gain, w_up, w_down, policy_gain, w_policy):
@@ -426,15 +476,27 @@
     vmem = pl.BlockSpec(memory_space=pltpu.VMEM)
     dma = pltpu.SemaphoreType.DMA
     half = jnp.bfloat16
+    operands = (
+        states,
+        member_of,
+        place.reshape(1, count),
+        norm_gain,
+        w_up,
+        w_down,
+        policy_gain.reshape(1, width),
+        w_policy,
+    )
     return pl.pallas_call(
         rollout_kernel,
         out_shape=(
             jax.ShapeDtypeStruct((count, width), half),
             jax.ShapeDtypeStruct((count, w_policy.shape[1]), half),
         ),
-        in_specs=[vmem] * 8,
+        in_specs=[pl.BlockSpec(memory_space=pltpu.HBM)] * 8,
         out_specs=(vmem, vmem),
         scratch_shapes=[
+            *(pltpu.VMEM(operand.shape, operand.dtype) for operand in operands),
+            dma((8,)),
             pltpu.VMEM((8, 2, count, width), half),
             pltpu.VMEM((8, 2, 8, 128), jnp.float32),
             pltpu.VMEM((8, 2, count, width), half),
@@ -445,15 +507,15 @@
             pltpu.VMEM((4, count, width), half),
             pltpu.VMEM((4, count, width), half),
             pltpu.VMEM((count, width), jnp.float32),
-            dma((2, 4, 8)),
-            dma((2, 8, 2)),
+            dma((3, 4, 8)),
+            dma((3, 8, 2)),
             dma((8,)),
             dma((8,)),
-            dma((4,)),
-            dma((4,)),
-            dma((4,)),
-            dma((4,)),
-            dma((4,)),
+            dma((4, 2)),
+            dma((4, 2)),
+            dma((4, 2)),
+            dma((4, 2)),
+            dma((4, 2)),
         ],
         compiler_params=pltpu.CompilerParams(
             collective_id=0, has_side_effects=True, vmem_limit_bytes=48 * 1024 * 1024
@@ -463,16 +525,7 @@
             bytes_accessed=8 * 1024 * 1024,
             transcendentals=16 * count * w_up.shape[2],
         ),
-    )(
-        states,
-        member_of,
-        place.reshape(1, count),
-        norm_gain,
-        w_up,
-        w_down,
-        policy_gain.reshape(1, width),
-        w_policy,
-    )
+    )(*operands)
 
 
 def solution(mesh):

time: 75.5 us -> 79.3 us (1.050)
  Pallas kernels: 67.5 us -> 71.3 us
    pallas_call x1, Pallas kernels: 67.5 us -> 71.3 us  [gathered(): pl.pallas_call(rollout_kernel, out_shape=(jax.ShapeDtypeStruct((count, wi...]
where the time goes in v2:
time: 79.3 us; the launch traced here: 79 us
  Pallas kernels  71.3 us (90%)
  local copies, waits for them, and re-layouts  7.02 us (9%)
    pallas_call x1, Pallas kernels, gathered(): pl.pallas_call(rollout_kernel, out_shape=(jax.ShapeDtypeStruct((count, wi...  71.3 us
    unnamed x19, local copies, waits for them, and re-layouts  7.02 us

profile of v2, /device:TPU:0, one launch (start us, length us, event | category | flops | bytes accessed | tf_op | source)
XLA Modules:
  0.0 79.0 jit_solution(8537879016705621041)
XLA Ops:
  0.6 0.0 copy-start.7
  0.6 0.6 copy-done.7
  1.3 0.0 copy-start.4
  1.3 0.0 copy-start.5
  1.3 0.0 copy-start.6
  1.3 0.1 copy.10.member_in
  1.4 0.6 copy-done.4
  2.0 0.0 copy-done.5
  2.0 0.0 copy-done.6
  2.0 0.0 copy-start
  2.0 1.2 %copy-done = bf16[1,1024,512]{2,1,0:T(8,128)(2,1)S(1)} copy-done((bf16[1,1024,512]{2,1,0:T(8,128)(2,1)S(1)}, bf16[1,1024,512]{2,1,0:T(8,128)(2,1)}, u32[]{:S(2)}) %copy-start) | copy-done | bytes 1048600
  3.2 0.0 copy-start.1
  3.2 1.2 %copy-done.1 = bf16[1,512,1024]{2,1,0:T(8,128)(2,1)S(1)} copy-done((bf16[1,512,1024]{2,1,0:T(8,128)(2,1)S(1)}, bf16[1,512,1024]{2,1,0:T(8,128)(2,1)}, u32[]{:S(2)}) %copy-start.1) | copy-done | bytes 1048600
  4.4 0.0 copy-start.2
  4.4 0.9 %copy-done.2 = bf16[128,1024]{1,0:T(8,128)(2,1)S(1)} copy-done((bf16[128,1024]{1,0:T(8,128)(2,1)S(1)}, bf16[128,1024]{1,0:T(8,128)(2,1)}, u32[]{:S(2)}) %copy-start.2) | copy-done | bytes 262168
  5.4 0.0 copy-start.3
  5.4 0.9 %copy-done.3 = bf16[1024,128]{1,0:T(8,128)(2,1)S(1)} copy-done((bf16[1024,128]{1,0:T(8,128)(2,1)S(1)}, bf16[1024,128]{1,0:T(8,128)(2,1)}, u32[]{:S(2)}) %copy-start.3) | copy-done | bytes 262168
  6.3 71.3 %shard_map.95 = (bf16[128,1024]{1,0:T(8,128)(2,1)S(1)}, bf16[128,128]{1,0:T(8,128)(2,1)S(1)}) custom-call(bf16[128,1024]{1,0:T(8,128)(2,1)S(1)} %copy-done.2, s32[128,1]{1,0:T(8,128)S(1)} %copy.10.member_in, s32[1,128]{1,0:T(1,128)S(1)} %bitcast.3, f32[2,1024]{1,0:T(2,128)S(1)} %copy-done.4, bf16[1,1024,512]{2,1,0:T(8,128)(2,1)S(1)} %copy-done, ...), custom_call_target="tpu_custom_call" | custom-call | flops 4294967296 | bytes 8388608 | tf_op jit(solution)/shard_map/pallas_call | solution.py:489
  77.6 0.7 copy.13
  78.3 0.6 copy.14
Async XLA Ops:
  0.6 0.7 copy-start.7
  1.3 0.7 copy-start.4
  1.3 0.7 copy-start.5
  1.3 0.7 copy-start.6
  2.0 1.2 %copy-start = (bf16[1,1024,512]{2,1,0:T(8,128)(2,1)S(1)}, bf16[1,1024,512]{2,1,0:T(8,128)(2,1)}, u32[]{:S(2)}) copy-start(bf16[1,1024,512]{2,1,0:T(8,128)(2,1)} %up_in.1) | copy-start | bytes 3145732
  3.2 1.2 %copy-start.1 = (bf16[1,512,1024]{2,1,0:T(8,128)(2,1)S(1)}, bf16[1,512,1024]{2,1,0:T(8,128)(2,1)}, u32[]{:S(2)}) copy-start(bf16[1,512,1024]{2,1,0:T(8,128)(2,1)} %down_in.1) | copy-start | bytes 3145732
  4.4 0.9 %copy-start.2 = (bf16[128,1024]{1,0:T(8,128)(2,1)S(1)}, bf16[128,1024]{1,0:T(8,128)(2,1)}, u32[]{:S(2)}) copy-start(bf16[128,1024]{1,0:T(8,128)(2,1)} %states_in.1) | copy-start | bytes 786436
  5.4 0.9 %copy-start.3 = (bf16[1024,128]{1,0:T(8,128)(2,1)S(1)}, bf16[1024,128]{1,0:T(8,128)(2,1)}, u32[]{:S(2)}) copy-start(bf16[1024,128]{1,0:T(8,128)(2,1)} %policy_in.1) | copy-start | bytes 786436
